TPU v7x, 32 devices: a whole 2x2x4 slice. The times are simulated.
32 devices in a mesh: dp: 4 (over y, x), fsdp: 8 (over z, core).
Axes of the slice: x: 2, y: 2, z: 4, core: 2. Of those that a mesh axis runs over, the one named last changes fastest.
Arguments:
- tokens: bfloat16 [1152, 77, 512], P(('dp', 'fsdp')), may hold values from -6 to 6
- segment_ids: int32 [1152, 77], P(('dp', 'fsdp')), may hold values from 0 to 3, never falling along the last dimension, each value on 1 to 40 neighbouring positions
- qkv_weight: bfloat16 [786432], P(('dp', 'fsdp')), may hold values from -0.25 to 0.25
- out_weight: bfloat16 [262144], P(('dp', 'fsdp')), may hold values from -0.75 to 0.75
- up_weight: bfloat16 [1048576], P(('dp', 'fsdp')), may hold values from -0.25 to 0.25
- up_bias: bfloat16 [2048], P(('dp', 'fsdp')), may hold values from -1.75 to 1.75
- down_weight: bfloat16 [1048576], P(('dp', 'fsdp')), may hold values from -0.125 to 0.125
- small_params: bfloat16 [4096], P(('dp', 'fsdp'))
- cotangent: bfloat16 [1152, 77, 512], P(('dp', 'fsdp')), may hold values from -6 to 6
Outputs:
- block_output: bfloat16 [1152, 77, 512], P(('dp', 'fsdp'))
- grad_tokens: bfloat16 [1152, 77, 512], P(('dp', 'fsdp'))
- grad_qkv_weight: float32 [786432], P(('dp', 'fsdp'))
- grad_out_weight: float32 [262144], P(('dp', 'fsdp'))
- grad_up_weight: float32 [1048576], P(('dp', 'fsdp'))
- grad_up_bias: float32 [2048], P(('dp', 'fsdp'))
- grad_down_weight: float32 [1048576], P(('dp', 'fsdp'))
- grad_small: float32 [4096], P(('dp', 'fsdp'))
Inputs may be any that keep to these rules, and one draw needn't show every extreme that they name: `segment_ids`: along each packed row the ids never fall; each id labels one run of 1 to 40 consecutive tokens.
All inputs are finite; a program needn't handle non-finite values.
Results may differ from a plain program's by a relative error of at most 0.0091.
Values may be sent and summed in bfloat16 or wider, within the bound.
A program may use at most 192 MiB of HBM per device.

v0:
```python
import functools

import jax
import jax.numpy as jnp
from jax import lax
from jax.experimental import pallas as pl
from jax.experimental.pallas import tpu as pltpu
from jax.sharding import PartitionSpec as P

bf16 = jnp.bfloat16
f32 = jnp.float32
HEADS = 8
HEAD_DIM = 64
GROUP = 4
NORM_EPS = 1e-05
GELU_SLOPE = 1.702
MASKED_SCORE = -1e30
MESH = pl.DeviceIdType.MESH
ROW_BLOCK = 6
UNROLL = 3
GATHER = (2, 3, 1, 3, 0, 3, 9)
REDUCE = (3, 2, 3, 6, 7, 9, 11, 11)
REDUCE_QKV = (1, 2, 3, 3, 4, 4, 5, 5, 6)
ARRAYS = ("qkv", "out", "up", "down")
HELD = ("qkv", "out", "up0", "down", "up1")


def nn(a, b):
    return lax.dot_general(a, b, (((1,), (0,)), ((), ())), preferred_element_type=f32)


def nt(a, b):
    return lax.dot_general(a, b, (((1,), (1,)), ((), ())), preferred_element_type=f32)


def tn(a, b):
    return lax.dot_general(a, b, (((0,), (0,)), ((), ())), preferred_element_type=f32)


def col_sum(v):
    return jnp.sum(v, axis=0, keepdims=True)


def lane_mean(v):
    return jnp.sum(v, axis=-1, keepdims=True) * (1.0 / v.shape[-1])


def normalize(x):
    xc = x - lane_mean(x)
    inv = lax.rsqrt(lane_mean(xc * xc) + NORM_EPS)
    return xc * inv, inv


def flip(index, bits):
    low, high = index % 2, index // 2
    if bits & 1:
        low = 1 - low
    if bits & 2:
        high = 1 - high
    return high * 2 + low


class Gather:
    def __init__(self, buf, send, recv, pos):
        self.buf, self.send, self.recv = buf, send, recv
        self.dp, self.z, self.c = pos

    def copy(self, index, slot, device):
        ref = self.buf.at[index]
        return pltpu.make_async_remote_copy(
            src_ref=ref, dst_ref=ref, send_sem=self.send.at[slot], recv_sem=self.recv.at[slot],
            device_id=device, device_id_type=MESH)

    def along_z(self, k, mine=True):
        z = self.z if mine else flip(self.z, k)
        return self.copy((self.dp, z, self.c), k - 1, (self.dp, flip(self.z, k) * 2 + self.c))

    def column(self, bit, mine=True):
        dp = self.dp if mine else flip(self.dp, bit)
        return self.copy((dp, slice(None), self.c), 2 + bit, (flip(self.dp, bit), self.z * 2 + self.c))

    def onward(self, bit, mine=True):
        other = 3 - bit
        dp = flip(self.dp, other) if mine else flip(self.dp, 3)
        half = pl.ds(0, 2) if bit == 2 else pl.ds(2, 2)
        return self.copy((dp, half, self.c), 4 + bit, (flip(self.dp, bit), self.z * 2 + self.c))

    def to_core(self, mine=True):
        c = self.c if mine else 1 - self.c
        return self.copy((slice(None), slice(None), c), 7, (self.dp, self.z * 2 + 1 - self.c))

    def start_z(self):
        for k in (1, 2, 3):
            self.along_z(k).start()

    def start_column(self):
        for k in (1, 2, 3):
            self.along_z(k, False).wait_recv()
        for bit in (1, 2):
            self.column(bit).start()

    def start_onward(self):
        for bit in (1, 2):
            self.column(3 - bit, False).wait_recv()
            self.onward(bit).start()

    def start_core(self):
        for bit in (1, 2):
            self.onward(bit, False).wait_recv()
        self.to_core().start()

    def finish(self):
        self.to_core(False).wait_recv()
        for k in (1, 2, 3):
            self.along_z(k).wait_send()
        for bit in (1, 2):
            self.column(bit).wait_send()
            self.onward(bit).wait_send()
        self.to_core().wait_send()


class EagerGather(Gather):
    def shard(self, k, bit, mine=True):
        dp = self.dp if mine else flip(self.dp, bit)
        return self.copy((dp, flip(self.z, k), self.c), 2 + bit * 4 + k - 1, (flip(self.dp, bit), self.z * 2 + self.c))

    def forward(self, k, mine=True):
        bit = 2 - k % 2
        dp = flip(self.dp, 3 - bit) if mine else flip(self.dp, 3)
        return self.copy((dp, flip(self.z, k), self.c), 13 + k, (flip(self.dp, bit), self.z * 2 + self.c))

    def core_column(self, bits, mine=True):
        c = self.c if mine else 1 - self.c
        return self.copy((flip(self.dp, bits), slice(None), c), 17 + bits, (self.dp, self.z * 2 + 1 - self.c))

    def start(self):
        for k in (1, 2, 3):
            self.along_z(k).start()
        for bit in (1, 2):
            self.shard(0, bit).start()

    def start_column(self, between=lambda: None):
        for k in (1, 2, 3):
            self.along_z(k, False).wait_recv()
            for bit in (1, 2):
                self.shard(k, bit).start()
            if k == 1:
                between()
        self.core_column(0).start()

    def start_onward(self):
        for k in (0, 1, 2, 3):
            bit = 2 - k % 2
            self.shard(k, 3 - bit, False).wait_recv()
            self.forward(k).start()
        for k in (0, 1, 2, 3):
            bit = 2 - k % 2
            self.shard(k, bit, False).wait_recv()
        for bit in (1, 2):
            self.core_column(bit).start()

    def start_core(self):
        for k in (0, 1, 2, 3):
            self.forward(k, False).wait_recv()
        self.core_column(3).start()

    def finish(self):
        for bits in (0, 1, 2, 3):
            self.core_column(bits, False).wait_recv()
        for k in (1, 2, 3):
            self.along_z(k).wait_send()
        for k in (0, 1, 2, 3):
            for bit in (1, 2):
                self.shard(k, bit).wait_send()
            self.forward(k).wait_send()
            self.core_column(k).wait_send()


class Scatter:
    def __init__(self, grad, half, from_core, from_dp, from_z, send, recv, pos, dtype=bf16):
        self.grad, self.half, self.from_core, self.from_dp, self.from_z = grad, half, from_core, from_dp, from_z
        self.send, self.recv, self.dtype = send, recv, dtype
        self.dp, self.z, self.c = pos

    def copy(self, src, dst, slot, device):
        return pltpu.make_async_remote_copy(
            src_ref=src, dst_ref=dst, send_sem=self.send.at[slot], recv_sem=self.recv.at[slot],
            device_id=device, device_id_type=MESH)

    def core_copy(self):
        return self.copy(self.half, self.from_core, 0, (self.dp, self.z * 2 + 1 - self.c))

    def dp_copy(self, step, bit, onward):
        half = bit - 1 if step == 0 else 2 - bit
        dp = flip(self.dp, 3 if onward else bit)
        return self.copy(self.from_core.at[dp, pl.ds(2 * half, 2)], self.from_dp.at[2 * step + onward, bit - 1],
                         1 + 2 * (2 * step + onward) + bit - 1, (flip(self.dp, bit), self.z * 2 + self.c))

    def z_copy(self, k):
        return self.copy(self.from_core.at[self.dp, flip(self.z, k)], self.from_z.at[k - 1], 6 + k,
                         (self.dp, flip(self.z, k) * 2 + self.c))

    def start_core(self, whole=None):
        if whole is not None:
            zero, one = whole[:, :, 0], whole[:, :, 1]
            self.grad[...] = jnp.where(self.c == 0, zero, one)
            self.half[...] = jnp.where(self.c == 0, one, zero).astype(self.dtype)
        self.core_copy().start()

    def own_part(self, *index):
        return self.grad[self.own(*index)].astype(f32)

    def own(self, *index):
        return index if len(self.grad.shape) == 4 else index + (slice(None),) * (2 - len(index)) + (self.c,)

    def start_dp(self):
        self.core_copy().wait_recv()
        for bit in (1, 2):
            for onward in (1, 0):
                at = (flip(self.dp, 3 if onward else bit), pl.ds(2 * (bit - 1), 2))
                self.from_core[at] = (self.own_part(*at) + self.from_core[at].astype(f32)).astype(self.dtype)
                self.dp_copy(0, bit, onward).start()

    def start_onward(self):
        for bit in (1, 2):
            first = 3 - bit
            self.dp_copy(0, first, 1).wait_recv()
            at = (flip(self.dp, bit), pl.ds(2 * (first - 1), 2))
            total = self.own_part(*at) + self.from_core[at].astype(f32)
            self.from_core[at] = (total + self.from_dp[1, first - 1].astype(f32)).astype(self.dtype)
            self.dp_copy(1, bit, 0).start()

    def start_z(self):
        for bit in (1, 2):
            self.dp_copy(0, bit, 0).wait_recv()
            self.dp_copy(1, bit, 0).wait_recv()
        for half in (0, 1):
            at = (self.dp, pl.ds(2 * half, 2))
            total = self.own_part(*at) + self.from_core[at].astype(f32)
            total += self.from_dp[0, half].astype(f32) + self.from_dp[2, 1 - half].astype(f32)
            self.grad[self.own(*at)] = total.astype(self.grad.dtype)
            self.from_core[at] = total.astype(self.dtype)
        for k in (1, 2, 3):
            self.z_copy(k).start()

    def finish(self):
        for k in (1, 2, 3):
            self.z_copy(k).wait_recv()
        total = self.own_part(self.dp, self.z)
        for k in (1, 2, 3):
            total += self.from_z[k - 1].astype(f32)
        self.core_copy().wait_send()
        for bit in (1, 2):
            self.dp_copy(0, bit, 0).wait_send()
            self.dp_copy(0, bit, 1).wait_send()
            self.dp_copy(1, bit, 0).wait_send()
        for k in (1, 2, 3):
            self.z_copy(k).wait_send()
        return total


class SmallScatter:
    def __init__(self, grad, from_fsdp, from_dp, send, recv, pos):
        self.grad, self.from_fsdp, self.from_dp, self.send, self.recv = grad, from_fsdp, from_dp, send, recv
        self.dp, self.z, self.c = pos

    def copy(self, src, dst, slot, device):
        return pltpu.make_async_remote_copy(
            src_ref=src, dst_ref=dst, send_sem=self.send.at[slot], recv_sem=self.recv.at[slot],
            device_id=device, device_id_type=MESH)

    def first(self, k):
        z, c = flip(self.z, k // 2), self.c if k % 2 == 0 else 1 - self.c
        return self.copy(self.grad.at[:, z, c], self.from_fsdp.at[k - 1], k - 1, (self.dp, z * 2 + c))

    def second(self, k):
        dp = flip(self.dp, k)
        return self.copy(self.grad.at[dp, self.z, self.c], self.from_dp.at[k - 1], 6 + k, (dp, self.z * 2 + self.c))

    def start(self):
        for k in range(1, 8):
            self.first(k).start()

    def pass_on(self):
        for k in range(1, 8):
            self.first(k).wait_recv()
        total = self.grad[:, self.z, self.c]
        for k in range(1, 8):
            total += self.from_fsdp[k - 1]
        self.grad[:, self.z, self.c] = total
        for k in (1, 2, 3):
            self.second(k).start()

    def finish(self):
        for k in (1, 2, 3):
            self.second(k).wait_recv()
        total = self.grad[self.dp, self.z, self.c] + self.from_dp[0] + self.from_dp[1] + self.from_dp[2]
        for k in range(1, 8):
            self.first(k).wait_send()
        for k in (1, 2, 3):
            self.second(k).wait_send()
        return total


def block_kernel(comm, R, S, SP, D, FF, *refs):
    RB, M, NB, FC, FH, NA = ROW_BLOCK, ROW_BLOCK * SP, R // ROW_BLOCK, FF // 8, FF // 2, R // UNROLL
    GW = GROUP * HEAD_DIM
    refs = list(refs)

    def take(n):
        out = refs[:n]
        del refs[:n]
        return out

    tok, seg, cot = take(3)
    shards = dict(zip(ARRAYS + ("small",), take(5)))
    out, gtok = take(2)
    if comm:
        shares = dict(zip(ARRAYS + ("small",), take(5)))
    else:
        grads = dict(zip(ARRAYS + ("small",), take(5)))
    tokv, cbuf, cs, QKV, ATT, PT, GM, ACC, GN, start, bias, smallv, gbias, gsmall = take(14)
    FL = ACC
    acc_up, acc_down = take(2)
    tsem, csem, osem = take(3)
    if comm:
        weights = dict(zip(HELD, take(5)))
        small_grad = take(1)[0]
        from_core, from_dp, from_z = (dict(zip(HELD, take(5))) for _ in range(3))
        small_fsdp, small_dp, gsend, grecv, ssend, srecv = take(6)
    else:
        weights = {k: shards[k] for k in ARRAYS if k != "up"}
        for i in (0, 1):
            weights["up%d" % i] = shards["up"].at[:, :, :, :, pl.ds(i * (FF // 2), FF // 2)]

    def loop(a, b, f):
        lax.fori_loop(a, b, f, 0)

    def staged(count, step, events):
        def body(i, carry):
            for at, act in events:
                if at < count:
                    pl.when(i == at)(act)
            return step(i, carry)

        loop(0, count, body)
        for at, act in events:
            if at >= count:
                act()

    def each(things, act):
        for thing in things:
            act(thing)

    def when(plan):
        return [(NA * at // 18, act) for at, act in plan]

    tok_copy = pltpu.make_async_copy(tok, tokv, tsem)
    tok_copy.start()

    def cot_copy(b, slot):
        return pltpu.make_async_copy(cot.at[pl.ds(b % NB * RB, RB)], cbuf.at[slot], csem.at[slot])

    def out_copy(b, slot):
        return pltpu.make_async_copy(cbuf.at[slot], out.at[pl.ds(b * RB, RB)], osem.at[slot])

    cot_copy(0, 0).start()
    if comm:
        dp = lax.axis_index("dp")
        fs = lax.axis_index("fsdp")
        pos = (dp, fs // 2, fs % 2)
        z, c = pos[1], pos[2]
        peers = [(flip(dp, k), fs) for k in (1, 2, 3)] + [(dp, flip(z, k) * 2 + c) for k in (1, 2, 3)]
        peers += [(dp, flip(z, k) * 2 + 1 - c) for k in (0, 1, 2, 3)]
        barrier = pltpu.get_barrier_semaphore()
        for peer in peers:
            pl.semaphore_signal(barrier, inc=1, device_id=peer, device_id_type=MESH)
        spread = small_grad.reshape(256, 128)
        for name in ARRAYS:
            rows = FF // 32 if name == "down" else 16
            src = shards[name]
            per = src.shape[0] // rows
            spread[0 : src.shape[0]] = src[...].astype(f32)
            for j in range(per):
                piece = spread[pl.ds(j, rows, stride=per), :].astype(bf16)
                half, at = divmod(128 * j, FH)
                held = weights["up%d" % half] if name == "up" else weights[name]
                held[dp, z, c, :, (at if name == "up" else 128 * j) : (at if name == "up" else 128 * j) + 128] = piece
        weights["qkv"][dp, z, c, :, 3 * D :] = shards["small"][...]
        gathers = {n: Gather(weights[n], gsend.at[i], grecv.at[i], pos) for i, n in enumerate(HELD)}
        gathers["qkv"] = EagerGather(weights["qkv"], gsend.at[0], grecv.at[0], pos)
        pl.semaphore_wait(barrier, len(peers))
        gathers["qkv"].start()
        rest = [gathers[n] for n in HELD[1:]]
        gathers["qkv"].start_column(lambda: each(rest[:2], Gather.start_z))

    cs[...] = jnp.zeros(cs.shape, bf16)
    sg = seg[...]
    st = jnp.zeros(sg.shape, jnp.int32)
    for v in range(1, 4):
        count = jnp.sum((sg < v).astype(f32), axis=1, keepdims=True).astype(jnp.int32)
        st = jnp.where(sg == v, count, st)
    st = jnp.concatenate([st, jnp.zeros((R, SP - S), jnp.int32)], axis=1)
    start[...] = jnp.concatenate([st] * GROUP, axis=1).reshape(R, 1, GROUP * SP)
    for ref in (acc_up, acc_down, gbias, gsmall):
        ref[...] = jnp.zeros(ref.shape, f32)
    tok_copy.wait()

    def load_x(b):
        for i in range(RB):
            cs[SP * i : SP * i + S] = tokv[b * RB + i]
        return cs[...].astype(f32)

    def rows_of(b):
        return pl.ds(pl.multiple_of(b * M, 16), M)

    def norm_one(b, carry):
        rows = rows_of(b)
        xh1 = normalize(load_x(b))[0]
        high = xh1.astype(bf16)
        ACC[rows] = high
        GN[rows] = (xh1 - high.astype(f32)).astype(bf16)
        return carry

    if comm:
        staged(NB, norm_one, [
            (0, gathers["qkv"].start_onward), (0, rest[2].start_z), (GATHER[0], lambda: each(rest[:2], Gather.start_column)),
            (GATHER[1], gathers["qkv"].start_core),
        ])
        gathers["qkv"].finish()
        wq = weights["qkv"]
        for s in range(32):
            piece = wq[s // 8, (s % 8) // 2, s % 2, :, 3 * D :].astype(f32)
            smallv[s // 4 : s // 4 + 1, 128 * (s % 4) : 128 * (s % 4) + 128] = piece[0:1]
        for s in range(0, 32, 2):
            two = [wq[s // 8, (s % 8) // 2, i, :, 3 * D : 3 * D + 64].astype(f32)[1:2] for i in (0, 1)]
            bias[:, 64 * s : 64 * s + 128] = jnp.concatenate(two, axis=1)
    else:
        lax.fori_loop(0, NB, norm_one, 0)
        bias[...] = shards["small"][8:12].astype(f32).reshape(1, FF)
        smallv[...] = shards["small"][0:8].astype(f32)

    def w_qkv(a, b):
        return weights["qkv"][:, :, :, :, a:b].reshape(D, b - a)

    sm = smallv[...]
    g1, c1, bq, bv, bo, g2, c2, bd = [sm[i : i + 1] for i in range(8)]
    scale = HEAD_DIM ** (-0.5)
    bkv = jnp.concatenate([jnp.zeros_like(bv), bv], axis=1)
    lane = lax.broadcasted_iota(jnp.int32, (1, GW), 1)
    head_mask = [(lane // HEAD_DIM == j).astype(f32).astype(bf16) for j in range(GROUP)]
    low_half = lax.broadcasted_iota(jnp.int32, (1, 128), 1) < HEAD_DIM

    def stack(v):
        return jnp.concatenate([v * head_mask[j] for j in range(GROUP)], axis=0)

    def project(b, carry):
        rows = rows_of(b)
        fl = ((ACC[rows].astype(f32) + GN[rows].astype(f32)) * g1 + c1).astype(bf16)
        QKV[rows, 0:D] = ((nn(fl, w_qkv(0, D)) + bq) * scale).astype(bf16)
        QKV[rows, D : 3 * D] = (nn(fl, w_qkv(D, 3 * D)) + bkv).astype(bf16)
        return carry

    kidx = lax.broadcasted_iota(jnp.int32, (SP, GROUP * SP), 0)
    qidx = lax.broadcasted_iota(jnp.int32, (1, GROUP * SP), 1)
    qidx = qidx - SP * sum((qidx >= SP * j).astype(jnp.int32) for j in range(1, GROUP))

    NG = HEADS // GROUP
    TILES = GW // 128

    def attend(i, carry):
        rs = [i * UNROLL + u for u in range(UNROLL)]
        rows = [pl.ds(pl.multiple_of(r * SP, 16), SP) for r in rs]
        todo = [(u, g) for u in range(UNROLL) for g in range(NG)]
        allowed = [(kidx >= start[r]) & (kidx <= qidx) for r in rs]
        ss = [nt(QKV[rows[u], D + GW * g : D + GW * g + GW], stack(QKV[rows[u], GW * g : GW * g + GW])) for u, g in todo]
        ss = [jnp.where(allowed[u], s, MASKED_SCORE) for (u, g), s in zip(todo, ss)]
        es = [jnp.exp(s - jnp.max(s, axis=0, keepdims=True)) for s in ss]
        ps = [(e * (1.0 / col_sum(e))).astype(bf16) for e in es]
        pqs = [p.T for p in ps]
        for (u, g), p in zip(todo, ps):
            PT[2 * rs[u] + g] = p
        for (u, g), pq in zip(todo, pqs):
            for t in range(TILES):
                at = GW * g + 128 * t
                o = nn(pq[2 * SP * t : 2 * SP * t + 2 * SP], QKV[rows[u], 2 * D + at : 2 * D + at + 128])
                ATT[rows[u], at : at + 128] = jnp.where(low_half, o[0:SP], o[SP : 2 * SP]).astype(bf16)
        return carry

    def feed(half, b, carry):
        step = half * NB + b
        slot = step % 2
        rows = rows_of(b)
        mid = load_x(b) + nn(ATT[rows], weights["out"][...].reshape(D, D)) + bo
        cot_copy(step, slot).wait()
        for i in range(RB):
            cs[SP * i : SP * i + S] = cbuf[slot, i]
        if half:

            @pl.when(b > 0)
            def _():
                out_copy(b - 1, 1 - slot).wait()

            @pl.when(b + 1 < NB)
            def _():
                cot_copy(b + 1, 1 - slot).start()

        else:
            cot_copy(b + 1, 1 - slot).start()
        xh2, r2 = normalize(mid)
        second = (xh2 * g2 + c2).astype(bf16)
        branch = cs[...]
        acts, gps = [], []
        for j in range(4):
            w_up = weights["up%d" % half][:, :, :, :, j * FC : (j + 1) * FC].reshape(D, FC)
            w_down = weights["down"][2 * half + j // 2, 2 * (j % 2) : 2 * (j % 2) + 2].reshape(FC, D)
            cols = slice((4 * half + j) * FC, (4 * half + j + 1) * FC)
            pre = nn(second, w_up) + bias[:, cols]
            s = 0.5 * jnp.tanh((0.5 * GELU_SLOPE) * pre) + 0.5
            a = pre * s
            gp = (nt(branch, w_down) * (s + GELU_SLOPE * a * (1.0 - s))).astype(bf16)
            gbias[:, cols] += col_sum(gp.astype(f32))
            acts.append(a.astype(bf16))
            gps.append(gp)
        act, gp = jnp.concatenate(acts, axis=1), jnp.concatenate(gps, axis=1)
        w_down = weights["down"][2 * half : 2 * half + 2].reshape(FH, D)
        w_up = weights["up%d" % half][...].reshape(D, FH)
        grown = nn(act, w_down)
        gn2 = nt(gp, w_up)
        acc_down[...] += tn(act, branch).reshape(acc_down.shape)
        acc_up[...] += tn(second, gp).reshape(acc_up.shape)
        if not half:
            ACC[rows] = grown.astype(bf16)
            GN[rows] = gn2.astype(bf16)
            return carry
        res = (mid + bd + ACC[rows].astype(f32) + grown).astype(bf16)
        for i in range(RB):
            cbuf[slot, i] = res[SP * i : SP * i + S]
        out_copy(b, slot).start()
        gn2 = gn2 + GN[rows].astype(f32)
        h = gn2 * g2
        up = branch.astype(f32)
        gm = up + r2 * (h - lane_mean(h) - xh2 * lane_mean(h * xh2))
        GM[rows] = gm.astype(bf16)
        gsmall[4:5] += col_sum(gm.astype(bf16).astype(f32))
        gsmall[5:6] += col_sum(gn2 * xh2)
        gsmall[6:7] += col_sum(gn2)
        gsmall[7:8] += col_sum(up)
        return carry

    def out_grad():
        return tn(ATT[...], GM[...]).reshape(4, 4, 2, D // 32, D)

    def attended_grad(b, carry):
        rows = rows_of(b)
        ATT[rows] = nt(GM[rows], weights["out"][...].reshape(D, D)).astype(bf16)
        return carry

    def attend_back(i, carry):
        rs = [i * UNROLL + u for u in range(UNROLL)]
        rows = [pl.ds(pl.multiple_of(r * SP, 16), SP) for r in rs]
        todo = [(u, g) for u in range(UNROLL) for g in range(NG)]
        gos = [stack(ATT[rows[u], GW * g : GW * g + GW]) for u, g in todo]
        dps = [nt(QKV[rows[u], 2 * D + GW * g : 2 * D + GW * g + GW], go) for (u, g), go in zip(todo, gos)]
        qs = [stack(QKV[rows[u], GW * g : GW * g + GW]) for u, g in todo]
        lows = [PT[2 * rs[u] + g] for u, g in todo]
        gvs = [nn(low, go).astype(bf16) for low, go in zip(lows, gos)]
        dss = []
        for low, dpr in zip(lows, dps):
            p = low.astype(f32)
            dss.append((p * (dpr - col_sum(p * dpr))).astype(bf16))
        gks = [nn(ds, q).astype(bf16) for ds, q in zip(dss, qs)]
        gqs = []
        for (u, g), ds in zip(todo, dss):
            dsq = ds.T
            for t in range(TILES):
                at = D + GW * g + 128 * t
                o = nn(dsq[2 * SP * t : 2 * SP * t + 2 * SP], QKV[rows[u], at : at + 128])
                gqs.append((jnp.where(low_half, o[0:SP], o[SP : 2 * SP]) * scale).astype(bf16))
        for r in rs:
            x = normalize(tokv[r].astype(f32))[0]
            FL[pl.ds(pl.multiple_of(r * SP, 16), S)] = (x * g1 + c1).astype(bf16)
        for n, (u, g) in enumerate(todo):
            for t in range(TILES):
                QKV[rows[u], GW * g + 128 * t : GW * g + 128 * t + 128] = gqs[n * TILES + t]
            QKV[rows[u], D + GW * g : D + GW * g + GW] = gks[n]
            QKV[rows[u], 2 * D + GW * g : 2 * D + GW * g + GW] = gvs[n]
        return carry

    def input_grad(b, carry):
        rows = rows_of(b)
        gq = QKV[rows]
        gn1 = nt(gq, w_qkv(0, 3 * D))
        xh1, r1 = normalize(load_x(b))
        h = gn1 * g1
        res = (GM[rows].astype(f32) + r1 * (h - lane_mean(h) - xh1 * lane_mean(h * xh1))).astype(bf16)
        for i in range(RB):
            tokv[b * RB + i] = res[SP * i : SP * i + S]
        gsmall[0:1] += col_sum(gn1 * xh1)
        gsmall[1:2] += col_sum(gn1)
        gsmall[2:3] += col_sum(gq[:, 0:D].astype(f32))
        gsmall[3:4] += col_sum(gq[:, 2 * D : 3 * D].astype(f32))
        return carry

    def qkv_grad(j):
        return tn(FL[...], QKV[:, j * D : (j + 1) * D]).reshape(4, 4, 2, D // 32, D)

    if not comm:
        loop(0, NB, project)
        loop(0, NA, attend)
        for half in (0, 1):
            loop(0, NB, functools.partial(feed, half))
            grads["up"][:, :, :, :, half * FH : (half + 1) * FH] = acc_up[...]
            grads["down"][2 * half : 2 * half + 2] = acc_down[...]
            if not half:
                acc_up[...] = jnp.zeros(acc_up.shape, f32)
                acc_down[...] = jnp.zeros(acc_down.shape, f32)
        grads["out"][...] = out_grad()
        loop(0, NB, attended_grad)
        out_copy(NB - 1, (2 * NB - 1) % 2).wait()
        loop(0, NA, attend_back)
        for j in range(3):
            grads["qkv"][:, :, :, :, j * D : (j + 1) * D] = qkv_grad(j)
        loop(0, NB, input_grad)
        tok_back = pltpu.make_async_copy(tokv, gtok, tsem)
        tok_back.start()
        tok_back.wait()
        grads["small"][0:8] = gsmall[...]
        grads["small"][8:12] = gbias[...].reshape(4, D)
        return

    staged(NB, project, [
        (GATHER[2], lambda: each(rest[:2], Gather.start_onward)), (GATHER[3], rest[2].start_column), (GATHER[3], rest[3].start_z),
    ])
    scat = {}
    for i, name in enumerate(HELD[1:]):
        scat[name] = Scatter(weights[name], weights[name].at[:, :, 1 - c], from_core[name], from_dp[name], from_z[name],
                             ssend.at[i], srecv.at[i], pos)
    for j in range(3):
        cols = pl.ds(j * D, D)
        own = acc_up.at[:, :, j // 2, :, pl.ds(j % 2 * D, D)]
        away = GN.at[pl.ds(j * D // 2, D // 2)].reshape(4, 4, D // 32, D)
        scat[j] = Scatter(own, away, from_core["qkv"].at[:, :, :, cols], from_dp["qkv"].at[:, :, :, :, cols],
                          from_z["qkv"].at[:, :, cols], ssend.at[4 + j], srecv.at[4 + j], pos)
    small = SmallScatter(small_grad, small_fsdp, small_dp, ssend.at[7], srecv.at[7], pos)
    out_s, up0_s, down_s, up1_s = (scat[n] for n in HELD[1:])
    staged(NA, attend, [
        (GATHER[4], lambda: each(rest[:2], Gather.start_core)), (GATHER[5], rest[2].start_onward),
        (GATHER[6], rest[2].start_core),
    ])
    for g in rest[:3]:
        g.finish()
    staged(NB, functools.partial(feed, 0), [(0, rest[3].start_column), (2, rest[3].start_onward), (3, rest[3].start_core)])
    rest[3].finish()
    weights["up0"][...] = acc_up[...].astype(bf16)
    weights["down"][0:2] = acc_down[...].astype(bf16)
    up0_s.start_core()
    acc_up[...] = jnp.zeros(acc_up.shape, f32)
    acc_down[...] = jnp.zeros(acc_down.shape, f32)
    staged(NB, functools.partial(feed, 1), [(1, up0_s.start_dp), (3, up0_s.start_onward), (5, up0_s.start_z)])
    weights["down"][2:4] = acc_down[...].astype(bf16)
    down_s.start_core()
    weights["up1"][...] = acc_up[...].astype(bf16)
    grad = out_grad().astype(bf16)
    loop(0, NB, attended_grad)
    weights["out"][...] = grad
    out_copy(NB - 1, (2 * NB - 1) % 2).wait()
    names = (down_s.start_dp, up1_s.start_core, out_s.start_core, up1_s.start_dp, out_s.start_dp,
             down_s.start_onward, up1_s.start_onward, out_s.start_onward)
    staged(NA, attend_back, list(zip(REDUCE, names)))
    for j in range(3):
        scat[j].start_core(qkv_grad(j))
        if j:
            scat[j - 1].start_dp()
    names = (scat[2].start_dp, down_s.start_z, scat[0].start_onward, up1_s.start_z, scat[1].start_onward, out_s.start_z,
             scat[2].start_onward, scat[0].start_z, scat[1].start_z)
    staged(NB, input_grad, list(zip(REDUCE_QKV, names)))
    tok_back = pltpu.make_async_copy(tokv, gtok, tsem)
    tok_back.start()
    gs = small_grad
    for s in range(32):
        row = s // 4
        gs[s // 8, (s % 8) // 2, s % 2, 0:1, 0:128] = gsmall[row : row + 1, 128 * (s % 4) : 128 * (s % 4) + 128]
        two = gbias[:, 128 * (s // 2) : 128 * (s // 2) + 128]
        gs[s // 8, (s % 8) // 2, s % 2, 1:2, 0:64] = two[:, 64 * (s % 2) : 64 * (s % 2) + 64]
    small.start()
    scat[2].start_z()

    def give(name, total, first=0):
        rows, cols = total.shape
        per = shares[name].shape[0] // rows
        for j in range(cols // 128):
            shares[name][pl.ds(first + j, rows, stride=per), :] = total[:, 128 * j : 128 * j + 128]

    give("up", up0_s.finish())
    give("down", down_s.finish())
    give("up", up1_s.finish(), FH // 128)
    give("out", out_s.finish())
    small.pass_on()
    for j in range(3):
        give("qkv", scat[j].finish(), j * D // 128)
    shares["small"][...] = small.finish()
    tok_back.wait()


def block_call(comm, tokens, segments, cotangent, pieces, FF):
    R, S, D = tokens.shape
    SP = (S + 15) // 16 * 16
    T, M = R * SP, ROW_BLOCK * SP
    V, dma = pltpu.VMEM, pltpu.SemaphoreType.DMA
    vm, hbm = pl.BlockSpec(memory_space=pltpu.VMEM), pl.BlockSpec(memory_space=pl.ANY)
    rows = {"qkv": (16, 3 * D), "out": (16, D), "up": (16, FF), "down": (FF // 32, D)}
    out_shape = [jax.ShapeDtypeStruct(tokens.shape, bf16)] * 2
    if comm:
        out_shape += [jax.ShapeDtypeStruct(p.shape, f32) for p in pieces[:4]]
        out_shape += [jax.ShapeDtypeStruct((8, 128), f32)]
    else:
        out_shape += [jax.ShapeDtypeStruct((4, 4, 2) + rows[n], f32) for n in ARRAYS]
        out_shape += [jax.ShapeDtypeStruct((12, D), f32)]
    scratch = [
        V((R, S, D), bf16), V((2, ROW_BLOCK, S, D), bf16), V((M, D), bf16),
        V((T, 3 * D), bf16), V((T, D), bf16), V((2 * R, SP, GROUP * SP), bf16), V((T, D), bf16),
        V((T, D), bf16), V((T, D), bf16), V((R, 1, GROUP * SP), jnp.int32), V((1, FF), f32), V((8, D), f32),
        V((1, FF), f32), V((8, D), f32), V((4, 4, 2, 16, FF // 2), f32),
        V((2, 4, 2, FF // 32, D), f32), dma, dma((2,)), dma((2,)),
    ]
    if comm:
        small = (8, 128)
        held = {"qkv": (16, 3 * D), "out": (16, D), "up0": (16, FF // 2), "down": (FF // 32, D), "up1": (16, FF // 2)}
        scratch += [V((4, 4, 2) + (held[n] if n != "qkv" else (16, 3 * D + 128)), bf16) for n in HELD]
        scratch += [V((4, 4, 2) + small, f32)]
        for lead in ((4, 4), (3, 2, 2), (3,)):
            scratch += [V(lead + held[n], bf16) for n in HELD]
        scratch += [V((7, 4) + small, f32), V((3,) + small, f32), dma((5, 21)), dma((5, 21)), dma((8, 10)), dma((8, 10))]
    params = dict(vmem_limit_bytes=63480 * 1000)
    if comm:
        params.update(collective_id=1, has_side_effects=True)
    return pl.pallas_call(
        functools.partial(block_kernel, comm, R, S, SP, D, FF),
        out_shape=out_shape,
        in_specs=[hbm, vm, hbm] + [vm] * 5,
        out_specs=[hbm, hbm] + [vm] * 5,
        scratch_shapes=scratch,
        compiler_params=pltpu.CompilerParams(**params),
    )(tokens, segments, cotangent, *pieces)


def hand_over_kernel(parts, *refs):
    n = len(parts)
    given, kept, held, into, away = refs[: n + 1], refs[n + 1 : 2 * n + 3], refs[2 * n + 3 : 3 * n + 3], refs[-2], refs[-1]
    spans, slot = [], 0
    for i, count in enumerate(parts):
        size = given[i].shape[0] // count
        for p in range(count):
            rows = pl.ds(p * size, size)
            first = pltpu.make_async_copy(given[i].at[rows], held[i].at[rows], into.at[slot])
            spans.append((first, pltpu.make_async_copy(held[i].at[rows], kept[i].at[rows], away.at[slot])))
            slot += 1
    for first, _ in spans:
        first.start()
    kept[n][...] = given[n][0:1]
    kept[n + 1][...] = given[n][1:2, 0 : kept[n + 1].shape[1]]
    for first, second in spans:
        first.wait()
        second.start()
    for _, second in spans:
        second.wait()


def hand_over(arrays, tile, count):
    n = len(arrays)
    parts = [6 if a.ndim == 3 else 1 for a in arrays]
    hbm, vm = pl.BlockSpec(memory_space=pl.ANY), pl.BlockSpec(memory_space=pltpu.VMEM)
    shapes = [jax.ShapeDtypeStruct(a.shape, a.dtype) for a in arrays]
    shapes += [jax.ShapeDtypeStruct((1, tile.shape[1]), f32), jax.ShapeDtypeStruct((1, count), f32)]
    sems = pltpu.SemaphoreType.DMA((sum(parts),))
    return pl.pallas_call(
        functools.partial(hand_over_kernel, parts), out_shape=shapes, in_specs=[hbm] * n + [vm],
        out_specs=[hbm] * n + [vm, vm], scratch_shapes=[pltpu.VMEM(a.shape, a.dtype) for a in arrays] + [sems, sems],
        compiler_params=pltpu.CompilerParams(vmem_limit_bytes=60 * 1024 * 1024),
    )(*arrays, tile)


def body(sizes, tokens, segment_ids, qkv_weight, out_weight, up_weight, up_bias, down_weight, small_params, cotangent):
    D = tokens.shape[2]
    n = sizes[0] * sizes[1]
    FF = up_bias.shape[0] * n
    flats = (qkv_weight, out_weight, up_weight, down_weight)
    if sizes == (4, 8):
        tile = jnp.pad(jnp.concatenate([small_params, up_bias]), (0, 16 * 128 - 192)).reshape(16, 128)
        o = block_call(True, tokens, segment_ids, cotangent, [f.reshape(-1, 128) for f in flats] + [tile], FF)
        o = hand_over(o[:6], o[6], up_bias.shape[0])
        shares = [v.reshape(-1) for v in o[2:]]
        return (o[0], o[1], shares[0], shares[1], shares[2], shares[5], shares[3], shares[4])
    axes = ("dp", "fsdp")

    def gather(v):
        return lax.all_gather(v, axes, axis=0, tiled=True)

    def scatter(v):
        return lax.psum_scatter(v.reshape(-1), axes, scatter_dimension=0, tiled=True)

    packed = lax.all_gather(jnp.concatenate([small_params, up_bias]), axes, axis=0, tiled=False)
    count = small_params.shape[0]
    tile = jnp.concatenate([packed[:, :count].reshape(8, D), packed[:, count:].reshape(4, D)])
    whole = [gather(f) for f in flats]
    shapes = ((4, 4, 2, 16, 3 * D), (4, 4, 2, 16, D), (4, 4, 2, 16, FF), (4, 4, 2, FF // 32, D))
    o = block_call(False, tokens, segment_ids, cotangent, [w.reshape(s) for w, s in zip(whole, shapes)] + [tile], FF)
    return (o[0], o[1], scatter(o[2]), scatter(o[3]), scatter(o[4]), scatter(o[6][8:12]), scatter(o[5]), scatter(o[6][0:8]))


def solution(mesh):
    rows, flat = P(("dp", "fsdp"), None, None), P(("dp", "fsdp"))
    in_specs = (rows, P(("dp", "fsdp"), None), flat, flat, flat, flat, flat, flat, rows)
    out_specs = (rows, rows, flat, flat, flat, flat, flat, flat)
    sizes = (mesh.shape["dp"], mesh.shape["fsdp"])
    return jax.shard_map(functools.partial(body, sizes), mesh=mesh, in_specs=in_specs, out_specs=out_specs, check_vma=False)
```

profile of v0, /device:TPU:0, one launch (start us, length us, event | category | flops | bytes accessed | tf_op | source)
XLA Modules:
  0.0 155.9 jit_solution(12439484911019950126)
XLA Ops:
  0.6 1.3 fusion.3.refs_7_
  1.9 147.2 %shard_map.152 = (bf16[36,77,512]{2,1,0:T(8,128)(2,1)}, bf16[36,77,512]{2,1,0:T(8,128)(2,1)}, f32[192,128]{1,0:T(8,128)}, f32[64,128]{1,0:T(8,128)}, f32[256,128...) custom-call(bf16[36,77,512]{2,1,0:T(8,128)(2,1)} %refs_0_.1, s32[36,77]{1,0:T(8,128)} %refs_1_.1, ...), custom_call_target="tpu_custom_call" | custom-call | tf_op jit(solution)/shard_map/pallas_call | solution.py:738
  149.1 6.6 %shard_map.153 = (bf16[36,77,512]{2,1,0:T(8,128)(2,1)}, bf16[36,77,512]{2,1,0:T(8,128)(2,1)}, f32[192,128]{1,0:T(8,128)}, f32[64,128]{1,0:T(8,128)}, f32[256,128...) custom-call(bf16[36,77,512]{2,1,0:T(8,128)(2,1)} %get-tuple-element.23.refs_0_, ...), custom_call_target="tpu_custom_call" | custom-call | tf_op jit(solution)/shard_map/pallas_call | solution.py:777
where the time goes:
time: 156 us
  Pallas kernels  154 us (99%)
    pallas_call x1, Pallas kernels, block_call(): pl.pallas_call(functools.partial(block_kernel, comm, R, S, SP, D, FF), ou...  147 us
    pallas_call x1, Pallas kernels, hand_over(): pl.pallas_call(functools.partial(hand_over_kernel, parts), out_shape=shap...  6.61 us

commit v1 on v0

--- a/solution.py
+++ b/solution.py
@@ -17,12 +17,14 @@
 MASKED_SCORE = -1e30
 MESH = pl.DeviceIdType.MESH
 ROW_BLOCK = 6
-UNROLL = 3
-GATHER = (2, 3, 1, 3, 0, 3, 9)
-REDUCE = (3, 2, 3, 6, 7, 9, 11, 11)
-REDUCE_QKV = (1, 2, 3, 3, 4, 4, 5, 5, 6)
+UNROLL = 4
+GATHER = (2, 3, 2, 4, 2, 8)
+FEED = (2, 4, 2, 4, 5)
+REDUCE = (0, 2, 3, 5, 7, 8)
+REDUCE_QKV = (0, 1, 1, 2, 2, 3, 4, 4, 5)
 ARRAYS = ("qkv", "out", "up", "down")
-HELD = ("qkv", "out", "up0", "down", "up1")
+HELD = ("qkv", "out", "up0", "down0", "up1", "down1")
+PART = {"down0": 0, "down1": 1}
 
 
 def nn(a, b):
@@ -61,9 +63,16 @@
 
 
 class Gather:
-    def __init__(self, buf, send, recv, pos):
-        self.buf, self.send, self.recv = buf, send, recv
+    def __init__(self, buf, send, recv, pos, part=None):
+        self.buf, self.send, self.recv, self.part = buf, send, recv, part
         self.dp, self.z, self.c = pos
+        self.nz = buf.shape[1]
+
+    def only(self, z, act):
+        if self.part is None:
+            act()
+        else:
+            pl.when(z // 2 == self.part)(act)
 
     def copy(self, index, slot, device):
         ref = self.buf.at[index]
@@ -73,7 +82,7 @@
 
     def along_z(self, k, mine=True):
         z = self.z if mine else flip(self.z, k)
-        return self.copy((self.dp, z, self.c), k - 1, (self.dp, flip(self.z, k) * 2 + self.c))
+        return self.copy((self.dp, z % self.nz, self.c), k - 1, (self.dp, flip(self.z, k) * 2 + self.c))
 
     def column(self, bit, mine=True):
         dp = self.dp if mine else flip(self.dp, bit)
@@ -82,7 +91,7 @@
     def onward(self, bit, mine=True):
         other = 3 - bit
         dp = flip(self.dp, other) if mine else flip(self.dp, 3)
-        half = pl.ds(0, 2) if bit == 2 else pl.ds(2, 2)
+        half = pl.ds(0 if bit == 2 else self.nz // 2, self.nz // 2)
         return self.copy((dp, half, self.c), 4 + bit, (flip(self.dp, bit), self.z * 2 + self.c))
 
     def to_core(self, mine=True):
@@ -91,11 +100,11 @@
 
     def start_z(self):
         for k in (1, 2, 3):
-            self.along_z(k).start()
+            self.only(self.z, self.along_z(k).start)
 
     def start_column(self):
         for k in (1, 2, 3):
-            self.along_z(k, False).wait_recv()
+            self.only(flip(self.z, k), self.along_z(k, False).wait_recv)
         for bit in (1, 2):
             self.column(bit).start()
 
@@ -112,7 +121,7 @@
     def finish(self):
         self.to_core(False).wait_recv()
         for k in (1, 2, 3):
-            self.along_z(k).wait_send()
+            self.only(self.z, self.along_z(k).wait_send)
         for bit in (1, 2):
             self.column(bit).wait_send()
             self.onward(bit).wait_send()
@@ -177,9 +186,10 @@
 
 
 class Scatter:
-    def __init__(self, grad, half, from_core, from_dp, from_z, send, recv, pos, dtype=bf16):
+    def __init__(self, grad, half, from_core, from_dp, from_z, send, recv, pos, part=None):
+        self.part, self.nz, self.dtype = part, from_core.shape[1], bf16
         self.grad, self.half, self.from_core, self.from_dp, self.from_z = grad, half, from_core, from_dp, from_z
-        self.send, self.recv, self.dtype = send, recv, dtype
+        self.send, self.recv = send, recv
         self.dp, self.z, self.c = pos
 
     def copy(self, src, dst, slot, device):
@@ -187,17 +197,26 @@
             src_ref=src, dst_ref=dst, send_sem=self.send.at[slot], recv_sem=self.recv.at[slot],
             device_id=device, device_id_type=MESH)
 
+    def only(self, z, act):
+        if self.part is None:
+            act()
+        else:
+            pl.when(z // 2 == self.part)(act)
+
+    def half_of(self, half):
+        return pl.ds(half * self.nz // 2, self.nz // 2)
+
     def core_copy(self):
         return self.copy(self.half, self.from_core, 0, (self.dp, self.z * 2 + 1 - self.c))
 
     def dp_copy(self, step, bit, onward):
         half = bit - 1 if step == 0 else 2 - bit
         dp = flip(self.dp, 3 if onward else bit)
-        return self.copy(self.from_core.at[dp, pl.ds(2 * half, 2)], self.from_dp.at[2 * step + onward, bit - 1],
+        return self.copy(self.from_core.at[dp, self.half_of(half)], self.from_dp.at[2 * step + onward, bit - 1],
                          1 + 2 * (2 * step + onward) + bit - 1, (flip(self.dp, bit), self.z * 2 + self.c))
 
     def z_copy(self, k):
-        return self.copy(self.from_core.at[self.dp, flip(self.z, k)], self.from_z.at[k - 1], 6 + k,
+        return self.copy(self.from_core.at[self.dp, flip(self.z, k) % self.nz], self.from_z.at[k - 1], 6 + k,
                          (self.dp, flip(self.z, k) * 2 + self.c))
 
     def start_core(self, whole=None):
@@ -217,7 +236,7 @@
         self.core_copy().wait_recv()
         for bit in (1, 2):
             for onward in (1, 0):
-                at = (flip(self.dp, 3 if onward else bit), pl.ds(2 * (bit - 1), 2))
+                at = (flip(self.dp, 3 if onward else bit), self.half_of(bit - 1))
                 self.from_core[at] = (self.own_part(*at) + self.from_core[at].astype(f32)).astype(self.dtype)
                 self.dp_copy(0, bit, onward).start()
 
@@ -225,7 +244,7 @@
         for bit in (1, 2):
             first = 3 - bit
             self.dp_copy(0, first, 1).wait_recv()
-            at = (flip(self.dp, bit), pl.ds(2 * (first - 1), 2))
+            at = (flip(self.dp, bit), self.half_of(first - 1))
             total = self.own_part(*at) + self.from_core[at].astype(f32)
             self.from_core[at] = (total + self.from_dp[1, first - 1].astype(f32)).astype(self.dtype)
             self.dp_copy(1, bit, 0).start()
@@ -235,28 +254,31 @@
             self.dp_copy(0, bit, 0).wait_recv()
             self.dp_copy(1, bit, 0).wait_recv()
         for half in (0, 1):
-            at = (self.dp, pl.ds(2 * half, 2))
+            at = (self.dp, self.half_of(half))
             total = self.own_part(*at) + self.from_core[at].astype(f32)
             total += self.from_dp[0, half].astype(f32) + self.from_dp[2, 1 - half].astype(f32)
             self.grad[self.own(*at)] = total.astype(self.grad.dtype)
             self.from_core[at] = total.astype(self.dtype)
         for k in (1, 2, 3):
-            self.z_copy(k).start()
-
-    def finish(self):
-        for k in (1, 2, 3):
-            self.z_copy(k).wait_recv()
-        total = self.own_part(self.dp, self.z)
-        for k in (1, 2, 3):
-            total += self.from_z[k - 1].astype(f32)
+            self.only(flip(self.z, k), self.z_copy(k).start)
+
+    def finish(self, use):
+        def whole():
+            for k in (1, 2, 3):
+                self.z_copy(k).wait_recv()
+            total = self.own_part(self.dp, self.z % self.nz)
+            for k in (1, 2, 3):
+                total += self.from_z[k - 1].astype(f32)
+            use(total)
+
+        self.only(self.z, whole)
         self.core_copy().wait_send()
         for bit in (1, 2):
             self.dp_copy(0, bit, 0).wait_send()
             self.dp_copy(0, bit, 1).wait_send()
             self.dp_copy(1, bit, 0).wait_send()
         for k in (1, 2, 3):
-            self.z_copy(k).wait_send()
-        return total
+            self.only(flip(self.z, k), self.z_copy(k).wait_send)
 
 
 class SmallScatter:
@@ -324,14 +346,12 @@
     acc_up, acc_down = take(2)
     tsem, csem, osem = take(3)
     if comm:
-        weights = dict(zip(HELD, take(5)))
+        weights = dict(zip(HELD, take(6)))
         small_grad = take(1)[0]
-        from_core, from_dp, from_z = (dict(zip(HELD, take(5))) for _ in range(3))
+        from_core, from_dp, from_z = (dict(zip(HELD, take(6))) for _ in range(3))
         small_fsdp, small_dp, gsend, grecv, ssend, srecv = take(6)
     else:
-        weights = {k: shards[k] for k in ARRAYS if k != "up"}
-        for i in (0, 1):
-            weights["up%d" % i] = shards["up"].at[:, :, :, :, pl.ds(i * (FF // 2), FF // 2)]
+        weights = shards
 
     def loop(a, b, f):
         lax.fori_loop(a, b, f, 0)
@@ -383,11 +403,22 @@
             spread[0 : src.shape[0]] = src[...].astype(f32)
             for j in range(per):
                 piece = spread[pl.ds(j, rows, stride=per), :].astype(bf16)
-                half, at = divmod(128 * j, FH)
-                held = weights["up%d" % half] if name == "up" else weights[name]
-                held[dp, z, c, :, (at if name == "up" else 128 * j) : (at if name == "up" else 128 * j) + 128] = piece
+                at = slice(128 * j, 128 * j + 128)
+                if name == "up":
+                    run, left = divmod(128 * j, 2 * FC)
+                    half, left = divmod(left, FC)
+                    weights["up%d" % half][dp, z, c, :, run * FC + left : run * FC + left + 128] = piece
+                elif name == "down":
+                    for part in (0, 1):
+
+                        @pl.when(z // 2 == part)
+                        def _(part=part, at=at, piece=piece):
+                            weights["down%d" % part][dp, z % 2, c, :, at] = piece
+
+                else:
+                    weights[name][dp, z, c, :, at] = piece
         weights["qkv"][dp, z, c, :, 3 * D :] = shards["small"][...]
-        gathers = {n: Gather(weights[n], gsend.at[i], grecv.at[i], pos) for i, n in enumerate(HELD)}
+        gathers = {n: Gather(weights[n], gsend.at[i], grecv.at[i], pos, PART.get(n)) for i, n in enumerate(HELD)}
         gathers["qkv"] = EagerGather(weights["qkv"], gsend.at[0], grecv.at[0], pos)
         pl.semaphore_wait(barrier, len(peers))
         gathers["qkv"].start()
@@ -424,7 +455,7 @@
 
     if comm:
         staged(NB, norm_one, [
-            (0, gathers["qkv"].start_onward), (0, rest[2].start_z), (GATHER[0], lambda: each(rest[:2], Gather.start_column)),
+            (0, gathers["qkv"].start_onward), (0, rest[2].start_z), (GATHER[0], lambda: each(rest[:3], Gather.start_column)),
             (GATHER[1], gathers["qkv"].start_core),
         ])
         gathers["qkv"].finish()
@@ -487,6 +518,16 @@
                 ATT[rows[u], at : at + 128] = jnp.where(low_half, o[0:SP], o[SP : 2 * SP]).astype(bf16)
         return carry
 
+    def up_part(half, j):
+        if comm:
+            return weights["up%d" % half][:, :, :, :, j * FC : (j + 1) * FC].reshape(D, FC)
+        return weights["up"][:, :, :, :, (2 * j + half) * FC : (2 * j + half + 1) * FC].reshape(D, FC)
+
+    def down_part(half, j):
+        if comm:
+            return weights["down%d" % half][j].reshape(FC, D)
+        return weights["down"][j, 2 * half : 2 * half + 2].reshape(FC, D)
+
     def feed(half, b, carry):
         step = half * NB + b
         slot = step % 2
@@ -512,9 +553,8 @@
         branch = cs[...]
         acts, gps = [], []
         for j in range(4):
-            w_up = weights["up%d" % half][:, :, :, :, j * FC : (j + 1) * FC].reshape(D, FC)
-            w_down = weights["down"][2 * half + j // 2, 2 * (j % 2) : 2 * (j % 2) + 2].reshape(FC, D)
-            cols = slice((4 * half + j) * FC, (4 * half + j + 1) * FC)
+            w_up, w_down = up_part(half, j), down_part(half, j)
+            cols = slice((2 * j + half) * FC, (2 * j + half + 1) * FC)
             pre = nn(second, w_up) + bias[:, cols]
             s = 0.5 * jnp.tanh((0.5 * GELU_SLOPE) * pre) + 0.5
             a = pre * s
@@ -523,8 +563,8 @@
             acts.append(a.astype(bf16))
             gps.append(gp)
         act, gp = jnp.concatenate(acts, axis=1), jnp.concatenate(gps, axis=1)
-        w_down = weights["down"][2 * half : 2 * half + 2].reshape(FH, D)
-        w_up = weights["up%d" % half][...].reshape(D, FH)
+        w_down = jnp.concatenate([down_part(half, j) for j in range(4)], axis=0)
+        w_up = jnp.concatenate([up_part(half, j) for j in range(4)], axis=1)
         grown = nn(act, w_down)
         gn2 = nt(gp, w_up)
         acc_down[...] += tn(act, branch).reshape(acc_down.shape)
@@ -610,8 +650,10 @@
         loop(0, NA, attend)
         for half in (0, 1):
             loop(0, NB, functools.partial(feed, half))
-            grads["up"][:, :, :, :, half * FH : (half + 1) * FH] = acc_up[...]
-            grads["down"][2 * half : 2 * half + 2] = acc_down[...]
+            for j in range(4):
+                at = (2 * j + half) * FC
+                grads["up"][:, :, :, :, at : at + FC] = acc_up[:, :, :, :, j * FC : (j + 1) * FC]
+            grads["down"][:, 2 * half : 2 * half + 2] = acc_down[...]
             if not half:
                 acc_up[...] = jnp.zeros(acc_up.shape, f32)
                 acc_down[...] = jnp.zeros(acc_down.shape, f32)
@@ -630,49 +672,57 @@
         return
 
     staged(NB, project, [
-        (GATHER[2], lambda: each(rest[:2], Gather.start_onward)), (GATHER[3], rest[2].start_column), (GATHER[3], rest[3].start_z),
+        (GATHER[2], lambda: each(rest[:3], Gather.start_onward)), (GATHER[3], lambda: each(rest[3:], Gather.start_z)),
     ])
     scat = {}
     for i, name in enumerate(HELD[1:]):
         scat[name] = Scatter(weights[name], weights[name].at[:, :, 1 - c], from_core[name], from_dp[name], from_z[name],
-                             ssend.at[i], srecv.at[i], pos)
+                             ssend.at[i], srecv.at[i], pos, PART.get(name))
     for j in range(3):
         cols = pl.ds(j * D, D)
         own = acc_up.at[:, :, j // 2, :, pl.ds(j % 2 * D, D)]
         away = GN.at[pl.ds(j * D // 2, D // 2)].reshape(4, 4, D // 32, D)
         scat[j] = Scatter(own, away, from_core["qkv"].at[:, :, :, cols], from_dp["qkv"].at[:, :, :, :, cols],
-                          from_z["qkv"].at[:, :, cols], ssend.at[4 + j], srecv.at[4 + j], pos)
-    small = SmallScatter(small_grad, small_fsdp, small_dp, ssend.at[7], srecv.at[7], pos)
-    out_s, up0_s, down_s, up1_s = (scat[n] for n in HELD[1:])
+                          from_z["qkv"].at[:, :, cols], ssend.at[5 + j], srecv.at[5 + j], pos)
+    small = SmallScatter(small_grad, small_fsdp, small_dp, ssend.at[8], srecv.at[8], pos)
+    out_s, up0_s, down0_s, up1_s, down_s = (scat[n] for n in HELD[1:])
+    first = (up0_s, down0_s)
     staged(NA, attend, [
-        (GATHER[4], lambda: each(rest[:2], Gather.start_core)), (GATHER[5], rest[2].start_onward),
-        (GATHER[6], rest[2].start_core),
+        (GATHER[4], lambda: each(rest[:3], Gather.start_core)), (GATHER[5], lambda: each(rest[3:], Gather.start_column)),
     ])
     for g in rest[:3]:
         g.finish()
-    staged(NB, functools.partial(feed, 0), [(0, rest[3].start_column), (2, rest[3].start_onward), (3, rest[3].start_core)])
-    rest[3].finish()
+    staged(NB, functools.partial(feed, 0), [
+        (FEED[0], lambda: each(rest[3:], Gather.start_onward)), (FEED[1], lambda: each(rest[3:], Gather.start_core)),
+    ])
+    for g in rest[3:]:
+        g.finish()
     weights["up0"][...] = acc_up[...].astype(bf16)
-    weights["down"][0:2] = acc_down[...].astype(bf16)
-    up0_s.start_core()
+    weights["down0"][...] = acc_down[...].astype(bf16)
+    each(first, Scatter.start_core)
     acc_up[...] = jnp.zeros(acc_up.shape, f32)
     acc_down[...] = jnp.zeros(acc_down.shape, f32)
-    staged(NB, functools.partial(feed, 1), [(1, up0_s.start_dp), (3, up0_s.start_onward), (5, up0_s.start_z)])
-    weights["down"][2:4] = acc_down[...].astype(bf16)
+    staged(NB, functools.partial(feed, 1), [
+        (FEED[2], lambda: each(first, Scatter.start_dp)), (FEED[3], lambda: each(first, Scatter.start_onward)),
+        (FEED[4], lambda: each(first, Scatter.start_z)),
+    ])
+    weights["down1"][...] = acc_down[...].astype(bf16)
     down_s.start_core()
     weights["up1"][...] = acc_up[...].astype(bf16)
+    up1_s.start_core()
     grad = out_grad().astype(bf16)
     loop(0, NB, attended_grad)
     weights["out"][...] = grad
+    out_s.start_core()
     out_copy(NB - 1, (2 * NB - 1) % 2).wait()
-    names = (down_s.start_dp, up1_s.start_core, out_s.start_core, up1_s.start_dp, out_s.start_dp,
+    names = (down_s.start_dp, up1_s.start_dp, out_s.start_dp,
              down_s.start_onward, up1_s.start_onward, out_s.start_onward)
     staged(NA, attend_back, list(zip(REDUCE, names)))
     for j in range(3):
         scat[j].start_core(qkv_grad(j))
         if j:
             scat[j - 1].start_dp()
-    names = (scat[2].start_dp, down_s.start_z, scat[0].start_onward, up1_s.start_z, scat[1].start_onward, out_s.start_z,
+    names = (down_s.start_z, scat[2].start_dp, up1_s.start_z, out_s.start_z, scat[0].start_onward, scat[1].start_onward,
              scat[2].start_onward, scat[0].start_z, scat[1].start_z)
     staged(NB, input_grad, list(zip(REDUCE_QKV, names)))
     tok_back = pltpu.make_async_copy(tokv, gtok, tsem)
@@ -686,19 +736,24 @@
     small.start()
     scat[2].start_z()
 
-    def give(name, total, first=0):
+    def give(name, total, place=lambda j: j):
         rows, cols = total.shape
         per = shares[name].shape[0] // rows
         for j in range(cols // 128):
-            shares[name][pl.ds(first + j, rows, stride=per), :] = total[:, 128 * j : 128 * j + 128]
-
-    give("up", up0_s.finish())
-    give("down", down_s.finish())
-    give("up", up1_s.finish(), FH // 128)
-    give("out", out_s.finish())
+            shares[name][pl.ds(place(j), rows, stride=per), :] = total[:, 128 * j : 128 * j + 128]
+
+    def give_up(half, total):
+        runs = FC // 128
+        give("up", total, lambda j: (2 * (j // runs) + half) * runs + j % runs)
+
+    up0_s.finish(functools.partial(give_up, 0))
+    down0_s.finish(functools.partial(give, "down"))
+    down_s.finish(functools.partial(give, "down"))
+    up1_s.finish(functools.partial(give_up, 1))
+    out_s.finish(functools.partial(give, "out"))
     small.pass_on()
     for j in range(3):
-        give("qkv", scat[j].finish(), j * D // 128)
+        scat[j].finish(functools.partial(give, "qkv", place=lambda i, j=j: j * D // 128 + i))
     shares["small"][...] = small.finish()
     tok_back.wait()
 
@@ -722,16 +777,20 @@
         V((T, 3 * D), bf16), V((T, D), bf16), V((2 * R, SP, GROUP * SP), bf16), V((T, D), bf16),
         V((T, D), bf16), V((T, D), bf16), V((R, 1, GROUP * SP), jnp.int32), V((1, FF), f32), V((8, D), f32),
         V((1, FF), f32), V((8, D), f32), V((4, 4, 2, 16, FF // 2), f32),
-        V((2, 4, 2, FF // 32, D), f32), dma, dma((2,)), dma((2,)),
+        V((4, 2, 2, FF // 32, D), f32), dma, dma((2,)), dma((2,)),
     ]
     if comm:
         small = (8, 128)
-        held = {"qkv": (16, 3 * D), "out": (16, D), "up0": (16, FF // 2), "down": (FF // 32, D), "up1": (16, FF // 2)}
-        scratch += [V((4, 4, 2) + (held[n] if n != "qkv" else (16, 3 * D + 128)), bf16) for n in HELD]
+        held = {"qkv": (16, 3 * D), "out": (16, D)}
+        for half in "01":
+            held.update({"up" + half: (16, FF // 2), "down" + half: (FF // 32, D)})
+        depth = {n: 2 if n in PART else 4 for n in HELD}
+        scratch += [V((4, depth[n], 2) + (held[n] if n != "qkv" else (16, 3 * D + 128)), bf16) for n in HELD]
         scratch += [V((4, 4, 2) + small, f32)]
-        for lead in ((4, 4), (3, 2, 2), (3,)):
-            scratch += [V(lead + held[n], bf16) for n in HELD]
-        scratch += [V((7, 4) + small, f32), V((3,) + small, f32), dma((5, 21)), dma((5, 21)), dma((8, 10)), dma((8, 10))]
+        scratch += [V((4, depth[n]) + held[n], bf16) for n in HELD]
+        scratch += [V((3, 2, depth[n] // 2) + held[n], bf16) for n in HELD]
+        scratch += [V((3,) + held[n], bf16) for n in HELD]
+        scratch += [V((7, 4) + small, f32), V((3,) + small, f32), dma((6, 21)), dma((6, 21)), dma((9, 10)), dma((9, 10))]
     params = dict(vmem_limit_bytes=63480 * 1000)
     if comm:
         params.update(collective_id=1, has_side_effects=True)

time: 156 us -> 149 us (0.955)
  Pallas kernels: 154 us -> 146 us
    pallas_call x1, Pallas kernels: 147 us -> 139 us  [block_call(): pl.pallas_call(functools.partial(block_kernel, comm, R, S, SP, D, FF), ou...]
where the time goes in v1:
time: 149 us; the launch traced here: 148 us
  Pallas kernels  146 us (98%)
    pallas_call x1, Pallas kernels, block_call(): pl.pallas_call(functools.partial(block_kernel, comm, R, S, SP, D, FF), ou...  139 us
    pallas_call x1, Pallas kernels, hand_over(): pl.pallas_call(functools.partial(hand_over_kernel, parts), out_shape=shap...  6.61 us

profile of v1, /device:TPU:0, one launch (start us, length us, event | category | flops | bytes accessed | tf_op | source)
XLA Modules:
  0.0 147.7 jit_solution(9111098427597414655)
XLA Ops:
  0.6 1.3 fusion.3.refs_7_
  1.9 139.0 %shard_map.152 = (bf16[36,77,512]{2,1,0:T(8,128)(2,1)}, bf16[36,77,512]{2,1,0:T(8,128)(2,1)}, f32[192,128]{1,0:T(8,128)}, f32[64,128]{1,0:T(8,128)}, f32[256,128...) custom-call(bf16[36,77,512]{2,1,0:T(8,128)(2,1)} %refs_0_.1, s32[36,77]{1,0:T(8,128)} %refs_1_.1, ...), custom_call_target="tpu_custom_call" | custom-call | tf_op jit(solution)/shard_map/pallas_call | solution.py:797
  140.9 6.6 %shard_map.153 = (bf16[36,77,512]{2,1,0:T(8,128)(2,1)}, bf16[36,77,512]{2,1,0:T(8,128)(2,1)}, f32[192,128]{1,0:T(8,128)}, f32[64,128]{1,0:T(8,128)}, f32[256,128...) custom-call(bf16[36,77,512]{2,1,0:T(8,128)(2,1)} %get-tuple-element.23.refs_0_, ...), custom_call_target="tpu_custom_call" | custom-call | tf_op jit(solution)/shard_map/pallas_call | solution.py:836

commit v2 on v1

--- a/solution.py
+++ b/solution.py
@@ -336,6 +336,8 @@
 
     tok, seg, cot = take(3)
     shards = dict(zip(ARRAYS + ("small",), take(5)))
+    if comm:
+        shards["bias"] = take(1)[0]
     out, gtok = take(2)
     if comm:
         shares = dict(zip(ARRAYS + ("small",), take(5)))
@@ -417,7 +419,11 @@
 
                 else:
                     weights[name][dp, z, c, :, at] = piece
-        weights["qkv"][dp, z, c, :, 3 * D :] = shards["small"][...]
+        row = lax.broadcasted_iota(jnp.int32, (16, 128), 0)
+        given, extra = shards["small"][...].astype(f32), shards["bias"][...].astype(f32)
+        extra = jnp.concatenate([extra, jnp.zeros((1, 128 - extra.shape[1]), f32)], axis=1)
+        tile = jnp.where(row == 0, given, jnp.where(row == 1, extra, 0.0))
+        weights["qkv"][dp, z, c, :, 3 * D :] = tile.astype(bf16)
         gathers = {n: Gather(weights[n], gsend.at[i], grecv.at[i], pos, PART.get(n)) for i, n in enumerate(HELD)}
         gathers["qkv"] = EagerGather(weights["qkv"], gsend.at[0], grecv.at[0], pos)
         pl.semaphore_wait(barrier, len(peers))
@@ -797,44 +803,36 @@
     return pl.pallas_call(
         functools.partial(block_kernel, comm, R, S, SP, D, FF),
         out_shape=out_shape,
-        in_specs=[hbm, vm, hbm] + [vm] * 5,
+        in_specs=[hbm, vm, hbm] + [vm] * len(pieces),
         out_specs=[hbm, hbm] + [vm] * 5,
         scratch_shapes=scratch,
         compiler_params=pltpu.CompilerParams(**params),
     )(tokens, segments, cotangent, *pieces)
 
 
-def hand_over_kernel(parts, *refs):
-    n = len(parts)
+def hand_over_kernel(n, *refs):
     given, kept, held, into, away = refs[: n + 1], refs[n + 1 : 2 * n + 3], refs[2 * n + 3 : 3 * n + 3], refs[-2], refs[-1]
-    spans, slot = [], 0
-    for i, count in enumerate(parts):
-        size = given[i].shape[0] // count
-        for p in range(count):
-            rows = pl.ds(p * size, size)
-            first = pltpu.make_async_copy(given[i].at[rows], held[i].at[rows], into.at[slot])
-            spans.append((first, pltpu.make_async_copy(held[i].at[rows], kept[i].at[rows], away.at[slot])))
-            slot += 1
-    for first, _ in spans:
-        first.start()
+    reads = [pltpu.make_async_copy(given[i], held[i], into.at[i]) for i in range(n)]
+    writes = [pltpu.make_async_copy(held[i], kept[i], away.at[i]) for i in range(n)]
+    for read in reads:
+        read.start()
     kept[n][...] = given[n][0:1]
     kept[n + 1][...] = given[n][1:2, 0 : kept[n + 1].shape[1]]
-    for first, second in spans:
-        first.wait()
-        second.start()
-    for _, second in spans:
-        second.wait()
+    for read, write in zip(reads, writes):
+        read.wait()
+        write.start()
+    for write in writes:
+        write.wait()
 
 
 def hand_over(arrays, tile, count):
     n = len(arrays)
-    parts = [6 if a.ndim == 3 else 1 for a in arrays]
     hbm, vm = pl.BlockSpec(memory_space=pl.ANY), pl.BlockSpec(memory_space=pltpu.VMEM)
     shapes = [jax.ShapeDtypeStruct(a.shape, a.dtype) for a in arrays]
     shapes += [jax.ShapeDtypeStruct((1, tile.shape[1]), f32), jax.ShapeDtypeStruct((1, count), f32)]
-    sems = pltpu.SemaphoreType.DMA((sum(parts),))
+    sems = pltpu.SemaphoreType.DMA((n,))
     return pl.pallas_call(
-        functools.partial(hand_over_kernel, parts), out_shape=shapes, in_specs=[hbm] * n + [vm],
+        functools.partial(hand_over_kernel, n), out_shape=shapes, in_specs=[hbm] * n + [vm],
         out_specs=[hbm] * n + [vm, vm], scratch_shapes=[pltpu.VMEM(a.shape, a.dtype) for a in arrays] + [sems, sems],
         compiler_params=pltpu.CompilerParams(vmem_limit_bytes=60 * 1024 * 1024),
     )(*arrays, tile)
@@ -846,8 +844,8 @@
     FF = up_bias.shape[0] * n
     flats = (qkv_weight, out_weight, up_weight, down_weight)
     if sizes == (4, 8):
-        tile = jnp.pad(jnp.concatenate([small_params, up_bias]), (0, 16 * 128 - 192)).reshape(16, 128)
-        o = block_call(True, tokens, segment_ids, cotangent, [f.reshape(-1, 128) for f in flats] + [tile], FF)
+        given = [f.reshape(-1, 128) for f in flats] + [small_params.reshape(1, -1), up_bias.reshape(1, -1)]
+        o = block_call(True, tokens, segment_ids, cotangent, given, FF)
         o = hand_over(o[:6], o[6], up_bias.shape[0])
         shares = [v.reshape(-1) for v in o[2:]]
         return (o[0], o[1], shares[0], shares[1], shares[2], shares[5], shares[3], shares[4])

time: 149 us -> 147 us (0.987)
  no operation moved by 1% of the time
where the time goes in v2:
time: 147 us; the launch traced here: 146 us
  Pallas kernels  145 us (99%)
    pallas_call x1, Pallas kernels, block_call(): pl.pallas_call(functools.partial(block_kernel, comm, R, S, SP, D, FF), ou...  139 us
    pallas_call x1, Pallas kernels, hand_over(): pl.pallas_call(functools.partial(hand_over_kernel, n), out_shape=shapes,...  5.81 us

profile of v2, /device:TPU:0, one launch (start us, length us, event | category | flops | bytes accessed | tf_op | source)
XLA Modules:
  0.0 145.7 jit_solution(2712634925319327884)
XLA Ops:
  0.6 139.1 %shard_map.152 = (bf16[36,77,512]{2,1,0:T(8,128)(2,1)}, bf16[36,77,512]{2,1,0:T(8,128)(2,1)}, f32[192,128]{1,0:T(8,128)}, f32[64,128]{1,0:T(8,128)}, f32[256,128...) custom-call(bf16[36,77,512]{2,1,0:T(8,128)(2,1)} %refs_0_.1, s32[36,77]{1,0:T(8,128)} %refs_1_.1, ...), custom_call_target="tpu_custom_call" | custom-call | tf_op jit(solution)/shard_map/pallas_call | solution.py:803
  139.7 5.8 %shard_map.153 = (bf16[36,77,512]{2,1,0:T(8,128)(2,1)}, bf16[36,77,512]{2,1,0:T(8,128)(2,1)}, f32[192,128]{1,0:T(8,128)}, f32[64,128]{1,0:T(8,128)}, f32[256,128...) custom-call(bf16[36,77,512]{2,1,0:T(8,128)(2,1)} %get-tuple-element.23.refs_0_, ...), custom_call_target="tpu_custom_call" | custom-call | tf_op jit(solution)/shard_map/pallas_call | solution.py:834

commit v3 on v2

--- a/solution.py
+++ b/solution.py
@@ -573,8 +573,9 @@
         w_up = jnp.concatenate([up_part(half, j) for j in range(4)], axis=1)
         grown = nn(act, w_down)
         gn2 = nt(gp, w_up)
-        acc_down[...] += tn(act, branch).reshape(acc_down.shape)
-        acc_up[...] += tn(second, gp).reshape(acc_up.shape)
+        for acc, term in ((acc_down, tn(act, branch)), (acc_up, tn(second, gp))):
+            before = jnp.where(b == 0, 0.0, acc[...]) if half else acc[...]
+            acc[...] = before + term.reshape(acc.shape)
         if not half:
             ACC[rows] = grown.astype(bf16)
             GN[rows] = gn2.astype(bf16)
@@ -660,9 +661,6 @@
                 at = (2 * j + half) * FC
                 grads["up"][:, :, :, :, at : at + FC] = acc_up[:, :, :, :, j * FC : (j + 1) * FC]
             grads["down"][:, 2 * half : 2 * half + 2] = acc_down[...]
-            if not half:
-                acc_up[...] = jnp.zeros(acc_up.shape, f32)
-                acc_down[...] = jnp.zeros(acc_down.shape, f32)
         grads["out"][...] = out_grad()
         loop(0, NB, attended_grad)
         out_copy(NB - 1, (2 * NB - 1) % 2).wait()
@@ -706,8 +704,6 @@
     weights["up0"][...] = acc_up[...].astype(bf16)
     weights["down0"][...] = acc_down[...].astype(bf16)
     each(first, Scatter.start_core)
-    acc_up[...] = jnp.zeros(acc_up.shape, f32)
-    acc_down[...] = jnp.zeros(acc_down.shape, f32)
     staged(NB, functools.partial(feed, 1), [
         (FEED[2], lambda: each(first, Scatter.start_dp)), (FEED[3], lambda: each(first, Scatter.start_onward)),
         (FEED[4], lambda: each(first, Scatter.start_z)),

time: 147 us -> 146 us (level)
  no operation moved by 1% of the time
where the time goes in v3:
time: 146 us; the launch traced here: 145 us
  Pallas kernels  145 us (99%)
    pallas_call x1, Pallas kernels, block_call(): pl.pallas_call(functools.partial(block_kernel, comm, R, S, SP, D, FF), ou...  139 us
    pallas_call x1, Pallas kernels, hand_over(): pl.pallas_call(functools.partial(hand_over_kernel, n), out_shape=shapes,...  5.81 us

profile of v3, /device:TPU:0, one launch (start us, length us, event | category | flops | bytes accessed | tf_op | source)
XLA Modules:
  0.0 145.4 jit_solution(6215861403522948669)
XLA Ops:
  0.6 138.8 %shard_map.152 = (bf16[36,77,512]{2,1,0:T(8,128)(2,1)}, bf16[36,77,512]{2,1,0:T(8,128)(2,1)}, f32[192,128]{1,0:T(8,128)}, f32[64,128]{1,0:T(8,128)}, f32[256,128...) custom-call(bf16[36,77,512]{2,1,0:T(8,128)(2,1)} %refs_0_.1, s32[36,77]{1,0:T(8,128)} %refs_1_.1, ...), custom_call_target="tpu_custom_call" | custom-call | tf_op jit(solution)/shard_map/pallas_call | solution.py:799
  139.5 5.8 %shard_map.153 = (bf16[36,77,512]{2,1,0:T(8,128)(2,1)}, bf16[36,77,512]{2,1,0:T(8,128)(2,1)}, f32[192,128]{1,0:T(8,128)}, f32[64,128]{1,0:T(8,128)}, f32[256,128...) custom-call(bf16[36,77,512]{2,1,0:T(8,128)(2,1)} %get-tuple-element.23.refs_0_, ...), custom_call_target="tpu_custom_call" | custom-call | tf_op jit(solution)/shard_map/pallas_call | solution.py:830
